TPU v7x, 1024 devices: a whole 4x8x16 slice. The times are simulated.
1024 devices in a mesh: fsdp: 64 (over z, y_lo), rep: 16 (over x, y_hi, core).
Axes of the slice: x: 4, y: 8 (y_hi: 2, y_lo: 4; y = y_hi * 4 + y_lo), z: 16, core: 2. Of those that a mesh axis runs over, the one named last changes fastest.
Arguments:
- tokens: bfloat16 [7168, 8192], P('rep'), may hold values from -6 to 6
- cotangent: bfloat16 [7168, 16384], P('rep', 'fsdp'), may hold values from -6 to 6
- codes: bfloat16 [8192, 16384], P('rep', 'fsdp'), may hold values from -127 to 127
- scales: bfloat16 [32, 16384], P('rep', 'fsdp'), may hold values from 4.9829483e-05 to 0.00039863586
Outputs:
- activation: bfloat16 [7168, 16384], P(('rep', 'fsdp'))
- weight_grad: float32 [8192, 16384], P('rep', 'fsdp')
All inputs are finite; a program needn't handle non-finite values.
Results may differ from a plain program's by a relative error of at most 0.015.
Values may be sent and summed in bfloat16 or wider, within the bound.
A program may use at most 64 MiB of HBM per device.

v0:
```python
import jax
import jax.numpy as jnp
from jax import lax
from jax.sharding import PartitionSpec as P

BLOCK_ROWS = 256


def dequant(code_blocks, scale_rows):
    weight = code_blocks.astype(jnp.float32) * scale_rows.astype(jnp.float32)[:, None, :]
    return weight.astype(jnp.bfloat16).reshape(-1, code_blocks.shape[2])


def per_device(tokens, cotangent, codes, scales):
    rows_tok = tokens.shape[0]
    cols = codes.shape[1]
    code_blocks = codes.reshape(-1, BLOCK_ROWS, cols)
    weight = dequant(
        lax.all_gather(code_blocks, "rep", axis=0, tiled=True),
        lax.all_gather(scales, "rep", axis=0, tiled=True),
    )
    columns = tokens
    up = jnp.dot(columns, weight, preferred_element_type=jnp.float32)
    sig = jax.nn.sigmoid(up)
    local_act = (up * sig).astype(jnp.bfloat16)
    activation = lax.all_to_all(local_act, "fsdp", split_axis=0, concat_axis=1, tiled=True)
    up_grad = (cotangent.astype(jnp.float32) * sig * (1.0 + up * (1.0 - sig))).astype(jnp.bfloat16)
    replicas = lax.axis_size("rep")
    columns = tokens
    summed = lax.psum_scatter(
        lax.dot_general(
            columns, up_grad, (((0,), (0,)), ((), ())), preferred_element_type=jnp.float32
        ).astype(jnp.bfloat16),
        "rep",
        scatter_dimension=0,
        tiled=True,
    ).astype(jnp.float32)
    count_all = rows_tok * replicas
    weight_grad = summed / jnp.sqrt(jnp.float32(count_all))
    return (activation, weight_grad)


def solution(mesh):
    return jax.shard_map(
        per_device,
        mesh=mesh,
        in_specs=(P("rep", None), P("rep", "fsdp"), P("rep", "fsdp"), P("rep", "fsdp")),
        out_specs=(P(("rep", "fsdp"), None), P("rep", "fsdp")),
        check_vma=False,
    )
```

profile of v0, /device:TPU:1, one launch (start us, length us, event | category | flops | bytes accessed | tf_op | source)
XLA Modules:
  0.0 258.0 jit_solution(11061528318526562912)
XLA Ops:
  7.2 0.0 all-gather.3.cloned.1.call-start
  7.2 0.7 all-gather.3.cloned.1.call-update
  7.9 0.0 reduce-scatter.2.cloned.1.call-start
  7.9 38.1 %all-gather = bf16[16,2,256]{2,1,0:T(2,128)(2,1)S(1)} all-gather(bf16[1,2,256]{2,1,0:T(2,128)(2,1)} %bitcast.16), channel_id=1, replica_groups=mesh['fsdp'=64,'rep'=16] {'rep'}, dimensions={0}, use_global_device_ids=true | all-gather | bytes 17408 | tf_op jit(solution)/shard_map/all_gather | solution.py:20
  46.0 68.9 %all-gather.3.cloned.1.call-done = bf16[32,256,256]{2,1,0:T(8,128)(2,1)} async-done(((bf16[2,256,256]{2,1,0:T(8,128)(2,1)}), bf16[32,256,256]{2,1,0:T(8,128)(2,1)}) %all-gather.3.cloned.1.call-update) | async-done | bytes 4194320 | tf_op jit(solution)/shard_map/all_gather | solution.py:19
  114.9 0.0 copy-start
  114.9 3.5 %multiply_convert_fusion = bf16[32,256,256]{2,1,0:T(8,128)(2,1)S(1)} fusion(bf16[32,256,256]{2,1,0:T(8,128)(2,1)} %all-gather.3.cloned.1.call-done, f32[32,256]{1,0:T(8,128)S(1)} %reshape.18), kind=kLoop, calls=%fused_computation.2 | loop fusion | flops 6291456 | bytes 8421376 | tf_op jit(solution)/shard_map/convert_element_type | solution.py:11
  118.4 0.8 copy-done
  119.2 0.0 copy-start.1
  119.2 2.1 multiply_convert_fusion.2
  121.3 0.0 copy-done.1
  121.3 4.5 %fusion = bf16[8192,256]{0,1:T(8,128)(2,1)} fusion(bf16[448,8192]{1,0:T(8,128)(2,1)S(1)} %copy-done, f32[448,256]{1,0:T(8,128)S(1)} %get-tuple-element.9, bf16[448,256]{1,0:T(8,128)(2,1)S(1)} %copy-done.1), kind=kOutput, calls=%fused_computation.1 | convolution fusion | flops 1882292224 | bytes 12222464 | tf_op jit(solution)/shard_map/dot_general | solution.py:31
  125.8 0.0 reduce-scatter.2.cloned.1.call-update
  125.8 0.1 all_to_all.14
  125.9 33.8 %all_to_all.19 = bf16[64,7,256]{2,1,0:T(8,128)(2,1)S(1)} all-to-all(bf16[64,7,256]{2,1,0:T(8,128)(2,1)S(1)} %all_to_all.14), channel_id=1, replica_groups=mesh['fsdp'=64,'rep'=16] {'fsdp'}, dimensions={0} | all-to-all | bytes 458752 | tf_op jit(solution)/shard_map/all_to_all | solution.py:26
  159.7 88.7 %reduce-scatter.2.cloned.1.call-done = bf16[512,256]{0,1:T(8,128)(2,1)} async-done(((bf16[8192,256]{0,1:T(8,128)(2,1)}), bf16[512,256]{0,1:T(8,128)(2,1)}) %reduce-scatter.2.cloned.1.call-update) | async-done | bytes 262160 | tf_op jit(solution)/shard_map/reduce_scatter | solution.py:30
  248.5 1.0 convert_multiply_fusion
  249.5 1.0 copy.8
  250.5 0.7 copy.10
  (1 shorter events, 0.0 us)
Async XLA Ops:
  7.2 107.7 %all-gather.3.cloned.1.call-start = ((), (), s32[]{:S(2)}) async-start(), calls=%async_computation.2 | async-start | bytes 4456448 | tf_op jit(solution)/shard_map/all_gather | solution.py:19
  7.9 240.6 %reduce-scatter.2.cloned.1.call-start = ((), (), s32[]{:S(2)}) async-start(), calls=%async_computation.3 | async-start | bytes 4456448 | tf_op jit(solution)/shard_map/reduce_scatter | solution.py:30
  114.9 4.3 %copy-start = (bf16[448,8192]{1,0:T(8,128)(2,1)S(1)}, bf16[448,8192]{1,0:T(8,128)(2,1)}, u32[]{:S(2)}) copy-start(bf16[448,8192]{1,0:T(8,128)(2,1)} %param.4) | copy-start | bytes 22020100
  119.2 2.1 copy-start.1
Sparse Core Ops, SparseCore 0:
  12.4 102.4 all-gather.2
  126.0 122.4 reduce-scatter.1
where the time goes:
time: 258 us
  waiting for transfers between devices  158 us (61%)
  blocking collectives  71.9 us (28%)
  between operations  14.1 us (5%)
  matrix products  6.57 us (3%)
  other arithmetic  4.49 us (2%)
  local copies, waits for them, and re-layouts  2.64 us (1%)
    reduce_scatter x1, waiting for transfers between devices, per_device(): lax.psum_scatter(lax.dot_general(columns, up_grad, (((0,), (0,)), ((), ()...  88.7 us
    all_gather x1, waiting for transfers between devices, per_device(): lax.all_gather(code_blocks, 'rep', axis=0, tiled=True)  68.9 us
    all_gather x1, blocking collectives, per_device(): lax.all_gather(scales, 'rep', axis=0, tiled=True)  38.1 us
    all_to_all x1, blocking collectives, per_device(): lax.all_to_all(local_act, 'fsdp', split_axis=0, concat_axis=1, tiled=True)  33.8 us
  transfers between devices with their start and end apart: 2, of which 2 were waited for; matrix products, arithmetic and copies ran while one was open for 0% of the time, Pallas kernels for 0%

commit v1 on v0

v1 whole, which is shorter than its diff:
```python
import jax
import jax.numpy as jnp
from jax import lax
from jax.experimental import pallas as pl
from jax.experimental.pallas import tpu as pltpu
from jax.sharding import PartitionSpec as P

MESH = pl.DeviceIdType.MESH
BF = jnp.bfloat16
F32 = jnp.float32
NX, NYL, NZ = 4, 4, 16
TOK, D, COLS, ROWS = 448, 8192, 256, 512
HALF = 128
BLOCKS = 8
OWN = 7
INV = 1.0 / (7168.0**0.5)


def body(
    tok, cot, codes, scales, act_o, wg_o,
    T2, CT, CD, W, PS, PR, UGT, AF, S1, S2, A, GK, GS, GR, YS, YR,
    lsem, tsem, trem, wys, wyr, wxs, wxr, pss, psr, gs, gr, gys, gyr, ays, ayr, azs, azr,
):
    f = lax.axis_index("fsdp")
    r = lax.axis_index("rep")
    z, yl = f // NYL, f % NYL
    x, h, c = r // 4, (r // 2) % 2, r % 2

    def rep_of(xx, hh, cc):
        return xx * 4 + hh * 2 + cc

    def at_x(k):
        return (x + k + NX) % NX

    step = (1, -1)
    nbr = [(f, rep_of(at_x(s), h, c)) for s in step]
    anti = (f, rep_of(x, 1 - h, c))
    sib = (f, rep_of(x, h, 1 - c))

    def ylo_peer(j):
        return (z * NYL + (yl + j) % NYL, r)

    def z_peer(i):
        return (((z + i) % NZ) * NYL + yl, r)

    def remote(src, dst, ss, rs, dev):
        return pltpu.make_async_remote_copy(
            src_ref=src, dst_ref=dst, send_sem=ss, recv_sem=rs, device_id=dev, device_id_type=MESH
        )

    sent = []

    def send(cp):
        cp.start()
        sent.append(cp)

    ld_codes = pltpu.make_async_copy(codes, CD, lsem.at[0])
    ld_codes.start()
    barrier = pltpu.get_barrier_semaphore()
    for dev in (nbr[0], nbr[1], anti, sib):
        pl.semaphore_signal(barrier, 1, device_id=dev, device_id_type=MESH)
    for j in range(1, NYL):
        pl.semaphore_signal(barrier, 1, device_id=ylo_peer(j), device_id_type=MESH)

    def greet(i, carry):
        pl.semaphore_signal(barrier, 1, device_id=z_peer(i), device_id_type=MESH)
        return carry

    lax.fori_loop(1, NZ, greet, 0)

    def tok_cols(b, cc):
        return tok.at[:, pl.ds(pl.multiple_of((2 * b + cc) * ROWS, ROWS), ROWS)]

    ld_tok = [pltpu.make_async_copy(tok_cols(b, c), T2.at[c, b], lsem.at[2 + b]) for b in range(BLOCKS)]
    for cp in ld_tok:
        cp.start()
    ld_cot = pltpu.make_async_copy(cot, CT.at[c], lsem.at[1])
    ld_cot.start()

    ld_codes.wait()
    b0 = x * 2 + h
    for p in range(2):
        for k in range(2):
            rows, cols = pl.ds(k * 256, 256), pl.ds(p * HALF, HALF)
            W[b0, p, rows, :] = (
                CD[rows, cols].astype(F32) * scales[pl.ds(k, 1), cols].astype(F32)
            ).astype(BF)

    pl.semaphore_wait(barrier, 4 + (NYL - 1) + (NZ - 1))

    def wpiece(xx, hh, p, q):
        return W.at[xx * 2 + hh, p, pl.ds(q * 256, 256), :]

    def w_y(p, q, mine=True):
        hh = h if mine else 1 - h
        ref = wpiece(x, hh, p, q)
        return remote(ref, ref, wys.at[p, q], wyr.at[p, q], anti)

    def w_x(p, k, d, t, mine=True):
        hh = h if k == 0 else 1 - h
        back = (0 if t < 2 else 1) + (0 if mine else 1)
        q = 1 - d if t == 1 else d
        ref = wpiece(at_x(-step[d] * back), hh, p, q)
        return remote(ref, ref, wxs.at[p, k, d, t], wxr.at[p, k, d, t], nbr[d])

    def w_x_got(p, k, d, t):
        w_x(p, k, d, t, mine=False).wait_recv()

    def forward(p, k):
        for d in range(2):
            w_x_got(p, k, d, 0)
            send(w_x(p, k, d, 2))

    for p in range(2):
        for q in range(2):
            send(w_y(p, q))
        for t in range(2):
            for d in range(2):
                send(w_x(p, 0, d, t))

    tok_out = [remote(tok_cols(b, 1 - c), T2.at[c, b], tsem.at[b], trem.at[b], sib) for b in range(BLOCKS)]
    tok_in = [remote(tok_cols(b, c), T2.at[1 - c, b], tsem.at[b], trem.at[b], sib) for b in range(BLOCKS)]
    for cp in tok_out:
        send(cp)
    send(remote(cot, CT.at[c], tsem.at[8], trem.at[8], sib))
    cot_in = remote(cot, CT.at[1 - c], tsem.at[8], trem.at[8], sib)

    def up_block(xx, hh, p, first=False):
        b = xx * 2 + hh
        w = W[b, p]
        for s in range(2):
            new = jnp.dot(T2[s, b], w, preferred_element_type=F32)
            if first:
                PS[p, s] = new
            else:
                PS[p, s] += new

    def anti_send(p, q):
        w_y(p, q, mine=False).wait_recv()
        send(w_x(p, 1, q, 0))
        send(w_x(p, 1, 1 - q, 1))

    def neighbours(p, k):
        hh = h if k == 0 else 1 - h
        for d in range(2):
            w_x_got(p, k, d, 1)
        for d in range(2):
            up_block(at_x(-step[d]), hh, p)

    def far(p, k):
        hh = h if k == 0 else 1 - h
        for d in range(2):
            w_x_got(p, k, d, 2)
        up_block(at_x(2), hh, p)

    partial = [remote(PS.at[p], PR.at[p], pss.at[p], psr.at[p], sib) for p in range(2)]

    forward(0, 0)
    forward(1, 0)
    anti_send(0, 0)
    for cp in ld_tok:
        cp.wait()
    for cp in tok_in:
        cp.wait_recv()
    for p in range(2):
        up_block(x, h, p, first=True)
    anti_send(0, 1)
    neighbours(0, 0)
    far(0, 0)
    up_block(x, 1 - h, 0)
    anti_send(1, 0)
    neighbours(1, 0)
    forward(0, 1)
    far(1, 0)
    anti_send(1, 1)
    up_block(x, 1 - h, 1)
    neighbours(0, 1)
    far(0, 1)
    send(partial[0])
    forward(1, 1)
    ld_cot.wait()
    cot_in.wait_recv()

    def gradient(p):
        partial[p].wait_recv()
        for s in range(2):
            up = PS[p, s] + PR[p, s]
            sig = jax.nn.sigmoid(up)
            g = CT[s, :, pl.ds(p * HALF, HALF)].astype(F32) * sig * (1.0 + up * (1.0 - sig))
            UGT[p, s] = g.T.astype(BF)

    def act_y(p, j, mine=True):
        to = (yl + j) % NYL
        frm = yl if mine else (yl - j + NYL) % NYL
        return remote(S1.at[p, to], S2.at[p, frm], ays.at[p, j], ayr.at[p, j], ylo_peer(j))

    def act_z(p, i, mine=True):
        to = (z + i) % NZ
        frm = z if mine else (z - i + NZ) % NZ
        return remote(S2.at[p, :, to], A.at[p, frm], azs.at[p, i], azr.at[p, i], z_peer(i))

    def activation_out(p):
        up = PS[p, c] + PR[p, c]
        AF[p, pl.ds(0, TOK), :] = up * jax.nn.sigmoid(up)
        AF[p, pl.ds(TOK, 8), :] = jnp.zeros((8, HALF), F32)
        for to in range(NYL):
            for zz in range(NZ):
                S1[p, to, zz] = AF[p, pl.ds(OWN * (zz * NYL + to), 8), :].astype(BF)
        for j in range(1, NYL):
            send(act_y(p, j))
        S2[p, yl] = S1[p, yl]

    def activation_z(p):
        for j in range(1, NYL):
            act_y(p, j, mine=False).wait_recv()

        def go(i, carry):
            act_z(p, i).start()
            return carry

        lax.fori_loop(1, NZ, go, 0)
        A[p, z] = S2[p, :, z]

    def activation_end(p):
        def got(i, carry):
            act_z(p, i, mine=False).wait_recv()
            return carry

        lax.fori_loop(1, NZ, got, 0)
        for zz in range(NZ):
            for y4 in range(NYL):
                col = (zz * NYL + y4) * COLS + p * HALF
                act_o[:, pl.ds(col, HALF)] = A[p, zz, y4][:OWN, :]

    def grad_block(p, xx, hh):
        b = xx * 2 + hh
        return jnp.dot(UGT[p, 0], T2[0, b], preferred_element_type=F32) + jnp.dot(
            UGT[p, 1], T2[1, b], preferred_element_type=F32
        )

    def g_x(p, k, d, t):
        return remote(GS.at[p, k, d, t], GR.at[p, k, d, t], gs.at[p, k, d, t], gr.at[p, k, d, t], nbr[d])

    def halves(v, q):
        return v[q * 64 : (q + 1) * 64, :]

    def scatter_first(p, k):
        hh = 1 - h if k == 0 else h
        g = grad_block(p, at_x(2), hh)
        for d in range(2):
            GS[p, k, d, 0] = halves(g, d).astype(BF)
            send(g_x(p, k, d, 0))
        for d in range(2):
            g = grad_block(p, at_x(step[d]), hh)
            GS[p, k, d, 1] = halves(g, 1 - d).astype(BF)
            send(g_x(p, k, d, 1))
            GK[p, k, d] = halves(g, d)
        g = grad_block(p, x, hh)
        for q in range(2):
            GK[p, k, 2 + q] = halves(g, q)

    def scatter_second(p, k):
        for d in range(2):
            g_x(p, k, d, 0).wait_recv()
            GS[p, k, d, 2] = (GK[p, k, d] + GR[p, k, d, 0].astype(F32)).astype(BF)
            send(g_x(p, k, d, 2))

    def scatter_sum(p, k, q):
        return GK[p, k, 2 + q] + GR[p, k, 1 - q, 1].astype(F32) + GR[p, k, q, 2].astype(F32)

    def scatter_got(p, k):
        for d in range(2):
            g_x(p, k, d, 1).wait_recv()
        for d in range(2):
            g_x(p, k, d, 2).wait_recv()

    g_y = [remote(YS.at[p], YR.at[p], gys.at[p], gyr.at[p], anti) for p in range(2)]

    def cross(p):
        scatter_got(p, 0)
        for q in range(2):
            YS[p, pl.ds(q * 64, 64), :] = scatter_sum(p, 0, q).astype(BF)
        send(g_y[p])

    def finish(p):
        scatter_got(p, 1)
        g_y[p].wait_recv()
        total = jnp.concatenate(
            [scatter_sum(p, 1, q) + YR[p, pl.ds(q * 64, 64), :].astype(F32) for q in range(2)], axis=0
        )
        wg_o[:, pl.ds(p * HALF, HALF)] = total.T * INV

    gradient(0)
    scatter_first(0, 0)
    activation_out(0)
    neighbours(1, 1)
    far(1, 1)
    send(partial[1])
    scatter_second(0, 0)
    gradient(1)
    scatter_first(1, 0)
    activation_out(1)
    scatter_first(0, 1)
    activation_z(0)
    cross(0)
    scatter_second(1, 0)
    scatter_first(1, 1)
    activation_z(1)
    scatter_second(0, 1)
    cross(1)
    scatter_second(1, 1)
    activation_end(0)
    finish(0)
    activation_end(1)
    finish(1)

    for cp in sent:
        cp.wait_send()

    def done(i, carry):
        for p in range(2):
            act_z(p, i).wait_send()
        return carry

    lax.fori_loop(1, NZ, done, 0)


def per_device(tokens, cotangent, codes, scales):
    dma = pltpu.SemaphoreType.DMA
    hbm = pl.BlockSpec(memory_space=pl.ANY)
    vmem = pl.BlockSpec(memory_space=pltpu.VMEM)
    return pl.pallas_call(
        body,
        out_shape=(
            jax.ShapeDtypeStruct((OWN, NZ * NYL * COLS), BF),
            jax.ShapeDtypeStruct((ROWS, COLS), F32),
        ),
        in_specs=[hbm, hbm, hbm, vmem],
        out_specs=(vmem, vmem),
        scratch_shapes=[
            pltpu.VMEM((2, BLOCKS, TOK, ROWS), BF),
            pltpu.VMEM((2, TOK, COLS), BF),
            pltpu.VMEM((ROWS, COLS), BF),
            pltpu.VMEM((BLOCKS, 2, ROWS, HALF), BF),
            pltpu.VMEM((2, 2, TOK, HALF), F32),
            pltpu.VMEM((2, 2, TOK, HALF), F32),
            pltpu.VMEM((2, 2, HALF, TOK), BF),
            pltpu.VMEM((2, TOK + 8, HALF), F32),
            pltpu.VMEM((2, NYL, NZ, 8, HALF), BF),
            pltpu.VMEM((2, NYL, NZ, 8, HALF), BF),
            pltpu.VMEM((2, NZ, NYL, 8, HALF), BF),
            pltpu.VMEM((2, 2, 4, 64, ROWS), F32),
            pltpu.VMEM((2, 2, 2, 3, 64, ROWS), BF),
            pltpu.VMEM((2, 2, 2, 3, 64, ROWS), BF),
            pltpu.VMEM((2, HALF, ROWS), BF),
            pltpu.VMEM((2, HALF, ROWS), BF),
            dma((2 + BLOCKS,)),
            dma((9,)), dma((9,)),
            dma((2, 2)), dma((2, 2)),
            dma((2, 2, 2, 3)), dma((2, 2, 2, 3)),
            dma((2,)), dma((2,)),
            dma((2, 2, 2, 3)), dma((2, 2, 2, 3)),
            dma((2,)), dma((2,)),
            dma((2, NYL)), dma((2, NYL)),
            dma((2, NZ)), dma((2, NZ)),
        ],
        compiler_params=pltpu.CompilerParams(
            collective_id=0, has_side_effects=True, vmem_limit_bytes=48 << 20
        ),
        name="panel",
    )(tokens, cotangent, codes, scales)


def solution(mesh):
    return jax.shard_map(
        per_device,
        mesh=mesh,
        in_specs=(P("rep", None), P("rep", "fsdp"), P("rep", "fsdp"), P("rep", "fsdp")),
        out_specs=(P(("rep", "fsdp"), None), P("rep", "fsdp")),
        check_vma=False,
    )
```

time: 258 us -> 76.8 us (0.30)
  waiting for transfers between devices: 158 us -> 0 us
  Pallas kernels: 0 us -> 71.9 us
  blocking collectives: 71.9 us -> 0 us
  between operations: 14.1 us -> 0.65 us
  matrix products: 6.57 us -> 0 us
  other arithmetic: 4.49 us -> 0 us
    reduce_scatter x1 -> x0, waiting for transfers between devices: 88.7 us -> none  [per_device(): lax.psum_scatter(lax.dot_general(columns, up_grad, (((0,), (0,)), ((), ()...]
    pallas_call x0 -> x1, Pallas kernels: none -> 71.9 us  [per_device(): pl.pallas_call(body, out_shape=(jax.ShapeDtypeStruct((OWN, NZ * NYL * COL...]
    all_gather x1 -> x0, waiting for transfers between devices: 68.9 us -> none  [per_device(): lax.all_gather(code_blocks, 'rep', axis=0, tiled=True)]
    all_gather x1 -> x0, blocking collectives: 38.1 us -> none  [per_device(): lax.all_gather(scales, 'rep', axis=0, tiled=True)]
    all_to_all x1 -> x0, blocking collectives: 33.8 us -> none  [per_device(): lax.all_to_all(local_act, 'fsdp', split_axis=0, concat_axis=1, tiled=True)]
    dot_general x2 -> x0, matrix products: 6.57 us -> none  [the longest x1 4.49 us: per_device(): lax.dot_general(columns, up_grad, (((0,), (0,)), ((), ())), preferred_ele...]
    convert_element_type x1 -> x0, other arithmetic: 3.49 us -> none  [dequant(): return weight.astype(jnp.bfloat16).reshape(-1, code_blocks.shape[2])]
  transfers between devices with their start and end apart: 2 -> 0, of which waited for: 2 -> 0; matrix products, arithmetic and copies ran while one was open for 0% -> 0% of each run, Pallas kernels for 0% -> 0%
where the time goes in v1:
time: 76.8 us; the launch traced here: 76.6 us
  Pallas kernels  71.9 us (94%)
  local copies, waits for them, and re-layouts  4.06 us (5%)
    pallas_call x1, Pallas kernels, per_device(): pl.pallas_call(body, out_shape=(jax.ShapeDtypeStruct((OWN, NZ * NYL * COL...  71.9 us
    unnamed x8, local copies, waits for them, and re-layouts  4.06 us

profile of v1, /device:TPU:1, one launch (start us, length us, event | category | flops | bytes accessed | tf_op | source)
XLA Modules:
  0.0 76.6 jit_solution(13098531982141169837)
XLA Ops:
  0.6 0.0 copy-start
  0.6 0.9 %copy-done = bf16[512,256]{1,0:T(8,128)(2,1)S(1)} copy-done((bf16[512,256]{1,0:T(8,128)(2,1)S(1)}, bf16[512,256]{1,0:T(8,128)(2,1)}, u32[]{:S(2)}) %copy-start) | copy-done | bytes 262168
  1.6 0.0 copy-start.1
  1.6 0.9 %copy-done.1 = bf16[448,256]{1,0:T(8,128)(2,1)S(1)} copy-done((bf16[448,256]{1,0:T(8,128)(2,1)S(1)}, bf16[448,256]{1,0:T(8,128)(2,1)}, u32[]{:S(2)}) %copy-start.1) | copy-done | bytes 229400
  2.5 0.0 copy-start.2
  2.5 0.7 copy-done.2
  3.2 71.9 %panel.1 = (bf16[7,16384]{1,0:T(8,128)(2,1)S(1)}, f32[512,256]{1,0:T(8,128)S(1)}) custom-call(bf16[448,8192]{1,0:T(8,128)(2,1)} %tok.1, bf16[448,256]{1,0:T(8,128)(2,1)S(1)} %copy-done.1, bf16[512,256]{1,0:T(8,128)(2,1)S(1)} %copy-done, bf16[2,256]{1,0:T(2,128)(2,1)S(1)} %copy-done.2), custom_call_target="tpu_custom_call" | custom-call | tf_op jit(solution)/shard_map/panel/pallas_call | solution.py:332
  75.1 0.7 copy.8
  75.8 0.8 %copy.9 = f32[512,256]{1,0:T(8,128)} copy(f32[512,256]{1,0:T(8,128)S(1)} %get-tuple-element.5) | data formatting | bytes 1048576
Async XLA Ops:
  0.6 1.0 %copy-start = (bf16[512,256]{1,0:T(8,128)(2,1)S(1)}, bf16[512,256]{1,0:T(8,128)(2,1)}, u32[]{:S(2)}) copy-start(bf16[512,256]{1,0:T(8,128)(2,1)} %codes.1) | copy-start | bytes 786436
  1.6 0.9 %copy-start.1 = (bf16[448,256]{1,0:T(8,128)(2,1)S(1)}, bf16[448,256]{1,0:T(8,128)(2,1)}, u32[]{:S(2)}) copy-start(bf16[448,256]{1,0:T(8,128)(2,1)} %cot.1) | copy-start | bytes 688132
  2.5 0.7 copy-start.2

commit v2 on v1

--- a/solution.py
+++ b/solution.py
@@ -18,8 +18,8 @@
 
 def body(
     tok, cot, codes, scales, act_o, wg_o,
-    T2, CT, CD, W, PS, PR, UGT, AF, S1, S2, A, GK, GS, GR, YS, YR,
-    lsem, tsem, trem, wys, wyr, wxs, wxr, pss, psr, gs, gr, gys, gyr, ays, ayr, azs, azr,
+    T2, CT, CD, SC, W, PS, PR, UGT, AF, S1, S2, A, GK, GS, GR, YS, YR,
+    lsem, tsem, trem, wys, wyr, wxs, wxr, pss, psr, gs, gr, gys, gyr, ays, ayr, azs, azr, zin,
 ):
     f = lax.axis_index("fsdp")
     r = lax.axis_index("rep")
@@ -56,37 +56,51 @@
 
     ld_codes = pltpu.make_async_copy(codes, CD, lsem.at[0])
     ld_codes.start()
+    ld_scales = pltpu.make_async_copy(scales, SC, lsem.at[2])
+    ld_scales.start()
     barrier = pltpu.get_barrier_semaphore()
     for dev in (nbr[0], nbr[1], anti, sib):
         pl.semaphore_signal(barrier, 1, device_id=dev, device_id_type=MESH)
     for j in range(1, NYL):
         pl.semaphore_signal(barrier, 1, device_id=ylo_peer(j), device_id_type=MESH)
 
-    def greet(i, carry):
-        pl.semaphore_signal(barrier, 1, device_id=z_peer(i), device_id_type=MESH)
-        return carry
-
-    lax.fori_loop(1, NZ, greet, 0)
+    def z_say(sem, k):
+        for s in (k, -k):
+            @pl.when((z + s >= 0) & (z + s < NZ))
+            def _():
+                pl.semaphore_signal(sem, 1, device_id=((z + s) * NYL + yl, r), device_id_type=MESH)
+
+    def z_count(k):
+        return jnp.where(z >= k, 1, 0) + jnp.where(z + k < NZ, 1, 0)
+
+    z_say(barrier, 1)
+
+    def z_round(k):
+        if k > 0:
+            pl.semaphore_wait(zin.at[k - 1], z_count(1 << (k - 1)))
+        if k < 4:
+            z_say(zin.at[k], 1 << k)
 
     def tok_cols(b, cc):
         return tok.at[:, pl.ds(pl.multiple_of((2 * b + cc) * ROWS, ROWS), ROWS)]
 
-    ld_tok = [pltpu.make_async_copy(tok_cols(b, c), T2.at[c, b], lsem.at[2 + b]) for b in range(BLOCKS)]
+    ld_tok = [pltpu.make_async_copy(tok_cols(b, c), T2.at[c, b], lsem.at[3 + b]) for b in range(BLOCKS)]
     for cp in ld_tok:
         cp.start()
     ld_cot = pltpu.make_async_copy(cot, CT.at[c], lsem.at[1])
     ld_cot.start()
 
     ld_codes.wait()
+    ld_scales.wait()
     b0 = x * 2 + h
     for p in range(2):
         for k in range(2):
             rows, cols = pl.ds(k * 256, 256), pl.ds(p * HALF, HALF)
             W[b0, p, rows, :] = (
-                CD[rows, cols].astype(F32) * scales[pl.ds(k, 1), cols].astype(F32)
+                CD[rows, cols].astype(F32) * SC[pl.ds(k, 1), cols].astype(F32)
             ).astype(BF)
 
-    pl.semaphore_wait(barrier, 4 + (NYL - 1) + (NZ - 1))
+    pl.semaphore_wait(barrier, 4 + (NYL - 1) + z_count(1))
 
     def wpiece(xx, hh, p, q):
         return W.at[xx * 2 + hh, p, pl.ds(q * 256, 256), :]
@@ -155,34 +169,37 @@
 
     partial = [remote(PS.at[p], PR.at[p], pss.at[p], psr.at[p], sib) for p in range(2)]
 
+    z_round(0)
     forward(0, 0)
     forward(1, 0)
     anti_send(0, 0)
+    z_round(1)
     for cp in ld_tok:
         cp.wait()
     for cp in tok_in:
         cp.wait_recv()
-    for p in range(2):
-        up_block(x, h, p, first=True)
+    up_block(x, h, 0, first=True)
     anti_send(0, 1)
+    z_round(2)
+    up_block(x, h, 1, first=True)
     neighbours(0, 0)
     far(0, 0)
+    anti_send(1, 0)
     up_block(x, 1 - h, 0)
-    anti_send(1, 0)
+    forward(0, 1)
     neighbours(1, 0)
-    forward(0, 1)
+    anti_send(1, 1)
+    z_round(3)
     far(1, 0)
-    anti_send(1, 1)
     up_block(x, 1 - h, 1)
     neighbours(0, 1)
+    forward(1, 1)
     far(0, 1)
     send(partial[0])
-    forward(1, 1)
     ld_cot.wait()
     cot_in.wait_recv()
 
     def gradient(p):
-        partial[p].wait_recv()
         for s in range(2):
             up = PS[p, s] + PR[p, s]
             sig = jax.nn.sigmoid(up)
@@ -290,29 +307,32 @@
         )
         wg_o[:, pl.ds(p * HALF, HALF)] = total.T * INV
 
+    partial[0].wait_recv()
+    activation_out(0)
     gradient(0)
-    scatter_first(0, 0)
-    activation_out(0)
     neighbours(1, 1)
     far(1, 1)
     send(partial[1])
+    scatter_first(0, 0)
+    z_round(4)
+    activation_z(0)
+    partial[1].wait_recv()
+    activation_out(1)
+    gradient(1)
     scatter_second(0, 0)
-    gradient(1)
     scatter_first(1, 0)
-    activation_out(1)
+    activation_z(1)
     scatter_first(0, 1)
-    activation_z(0)
     cross(0)
     scatter_second(1, 0)
     scatter_first(1, 1)
-    activation_z(1)
     scatter_second(0, 1)
     cross(1)
     scatter_second(1, 1)
+    finish(0)
     activation_end(0)
-    finish(0)
+    finish(1)
     activation_end(1)
-    finish(1)
 
     for cp in sent:
         cp.wait_send()
@@ -325,22 +345,42 @@
     lax.fori_loop(1, NZ, done, 0)
 
 
+def hand_over(act, wg, act_o, wg_o, act_v, wg_v, sem):
+    into = [
+        pltpu.make_async_copy(wg, wg_v, sem.at[0]),
+        pltpu.make_async_copy(act, act_v, sem.at[1]),
+    ]
+    out = [
+        pltpu.make_async_copy(wg_v, wg_o, sem.at[2]),
+        pltpu.make_async_copy(act_v, act_o, sem.at[3]),
+    ]
+    for cp in into:
+        cp.start()
+    for arrived, cp in zip(into, out):
+        arrived.wait()
+        cp.start()
+    for cp in out:
+        cp.wait()
+
+
 def per_device(tokens, cotangent, codes, scales):
     dma = pltpu.SemaphoreType.DMA
-    hbm = pl.BlockSpec(memory_space=pl.ANY)
+    hbm = pl.BlockSpec(memory_space=pltpu.HBM)
     vmem = pl.BlockSpec(memory_space=pltpu.VMEM)
-    return pl.pallas_call(
+    out_shape = (
+        jax.ShapeDtypeStruct((OWN, NZ * NYL * COLS), BF),
+        jax.ShapeDtypeStruct((ROWS, COLS), F32),
+    )
+    act, wg = pl.pallas_call(
         body,
-        out_shape=(
-            jax.ShapeDtypeStruct((OWN, NZ * NYL * COLS), BF),
-            jax.ShapeDtypeStruct((ROWS, COLS), F32),
-        ),
-        in_specs=[hbm, hbm, hbm, vmem],
+        out_shape=out_shape,
+        in_specs=[hbm, hbm, hbm, hbm],
         out_specs=(vmem, vmem),
         scratch_shapes=[
             pltpu.VMEM((2, BLOCKS, TOK, ROWS), BF),
             pltpu.VMEM((2, TOK, COLS), BF),
             pltpu.VMEM((ROWS, COLS), BF),
+            pltpu.VMEM((2, COLS), BF),
             pltpu.VMEM((BLOCKS, 2, ROWS, HALF), BF),
             pltpu.VMEM((2, 2, TOK, HALF), F32),
             pltpu.VMEM((2, 2, TOK, HALF), F32),
@@ -354,7 +394,7 @@
             pltpu.VMEM((2, 2, 2, 3, 64, ROWS), BF),
             pltpu.VMEM((2, HALF, ROWS), BF),
             pltpu.VMEM((2, HALF, ROWS), BF),
-            dma((2 + BLOCKS,)),
+            dma((3 + BLOCKS,)),
             dma((9,)), dma((9,)),
             dma((2, 2)), dma((2, 2)),
             dma((2, 2, 2, 3)), dma((2, 2, 2, 3)),
@@ -363,12 +403,26 @@
             dma((2,)), dma((2,)),
             dma((2, NYL)), dma((2, NYL)),
             dma((2, NZ)), dma((2, NZ)),
+            pltpu.SemaphoreType.REGULAR((4,)),
         ],
         compiler_params=pltpu.CompilerParams(
-            collective_id=0, has_side_effects=True, vmem_limit_bytes=48 << 20
+            collective_id=0, has_side_effects=True, vmem_limit_bytes=61 << 20
         ),
         name="panel",
     )(tokens, cotangent, codes, scales)
+    return pl.pallas_call(
+        hand_over,
+        out_shape=out_shape,
+        in_specs=[hbm, hbm],
+        out_specs=(hbm, hbm),
+        scratch_shapes=[
+            pltpu.VMEM((OWN, NZ * NYL * COLS), BF),
+            pltpu.VMEM((ROWS, COLS), F32),
+            dma((4,)),
+        ],
+        compiler_params=pltpu.CompilerParams(vmem_limit_bytes=61 << 20),
+        name="hand_over",
+    )(act, wg)
 
 
 def solution(mesh):

time: 76.8 us -> 68 us (0.89)
  Pallas kernels: 71.9 us -> 67.2 us
  local copies, waits for them, and re-layouts: 4.06 us -> 0 us
    pallas_call x1 -> x2, Pallas kernels: 71.9 us -> 67.2 us  [the longest x1 65.2 us: per_device(): pl.pallas_call(body, out_shape=out_shape, in_specs=[hbm, hbm, hbm, hbm],...]
    unnamed x8 -> x0, local copies, waits for them, and re-layouts: 4.06 us -> none
where the time goes in v2:
time: 68 us; the launch traced here: 67.8 us
  Pallas kernels  67.2 us (99%)
    pallas_call x1, Pallas kernels, per_device(): pl.pallas_call(body, out_shape=out_shape, in_specs=[hbm, hbm, hbm, hbm],...  65.2 us
    pallas_call x1, Pallas kernels, per_device(): pl.pallas_call(hand_over, out_shape=out_shape, in_specs=[hbm, hbm], out_s...  1.95 us

profile of v2, /device:TPU:1, one launch (start us, length us, event | category | flops | bytes accessed | tf_op | source)
XLA Modules:
  0.0 67.8 jit_solution(3654023834020827038)
XLA Ops:
  0.6 65.2 %panel.1 = (bf16[7,16384]{1,0:T(8,128)(2,1)}, f32[512,256]{1,0:T(8,128)}) custom-call(bf16[448,8192]{1,0:T(8,128)(2,1)} %tok.1, bf16[448,256]{1,0:T(8,128)(2,1)} %cot.1, bf16[512,256]{1,0:T(8,128)(2,1)} %codes.1, bf16[2,256]{1,0:T(2,128)(2,1)} %scales.1), custom_call_target="tpu_custom_call" | custom-call | tf_op jit(solution)/shard_map/panel/pallas_call | solution.py:374
  65.9 2.0 %hand_over.1 = (bf16[7,16384]{1,0:T(8,128)(2,1)}, f32[512,256]{1,0:T(8,128)}) custom-call(bf16[7,16384]{1,0:T(8,128)(2,1)} %get-tuple-element.4.act, f32[512,256]{1,0:T(8,128)} %get-tuple-element.5.wg), custom_call_target="tpu_custom_call" | custom-call | tf_op jit(solution)/shard_map/hand_over/pallas_call | solution.py:413

commit v3 on v2

--- a/solution.py
+++ b/solution.py
@@ -211,10 +211,13 @@
         frm = yl if mine else (yl - j + NYL) % NYL
         return remote(S1.at[p, to], S2.at[p, frm], ays.at[p, j], ayr.at[p, j], ylo_peer(j))
 
-    def act_z(p, i, mine=True):
+    def act_z(p, i):
         to = (z + i) % NZ
-        frm = z if mine else (z - i + NZ) % NZ
-        return remote(S2.at[p, :, to], A.at[p, frm], azs.at[p, i], azr.at[p, i], z_peer(i))
+        return remote(S2.at[p, :, to], A.at[p, z], azs.at[p], azr.at[p], z_peer(i))
+
+    def act_z_all(p):
+        part = A.at[p, pl.ds(0, NZ - 1)]
+        return remote(part, part, azs.at[p], azr.at[p], sib)
 
     def activation_out(p):
         up = PS[p, c] + PR[p, c]
@@ -239,11 +242,7 @@
         A[p, z] = S2[p, :, z]
 
     def activation_end(p):
-        def got(i, carry):
-            act_z(p, i, mine=False).wait_recv()
-            return carry
-
-        lax.fori_loop(1, NZ, got, 0)
+        act_z_all(p).wait_recv()
         for zz in range(NZ):
             for y4 in range(NYL):
                 col = (zz * NYL + y4) * COLS + p * HALF
@@ -337,12 +336,8 @@
     for cp in sent:
         cp.wait_send()
 
-    def done(i, carry):
-        for p in range(2):
-            act_z(p, i).wait_send()
-        return carry
-
-    lax.fori_loop(1, NZ, done, 0)
+    for p in range(2):
+        act_z_all(p).wait_send()
 
 
 def hand_over(act, wg, act_o, wg_o, act_v, wg_v, sem):
@@ -402,7 +397,7 @@
             dma((2, 2, 2, 3)), dma((2, 2, 2, 3)),
             dma((2,)), dma((2,)),
             dma((2, NYL)), dma((2, NYL)),
-            dma((2, NZ)), dma((2, NZ)),
+            dma((2,)), dma((2,)),
             pltpu.SemaphoreType.REGULAR((4,)),
         ],
         compiler_params=pltpu.CompilerParams(

time: 68 us -> 67.3 us (0.990)
  Pallas kernels: 67.2 us -> 66.5 us
where the time goes in v3:
time: 67.3 us; the launch traced here: 67.2 us
  Pallas kernels  66.5 us (99%)
    pallas_call x1, Pallas kernels, per_device(): pl.pallas_call(body, out_shape=out_shape, in_specs=[hbm, hbm, hbm, hbm],...  64.6 us
    pallas_call x1, Pallas kernels, per_device(): pl.pallas_call(hand_over, out_shape=out_shape, in_specs=[hbm, hbm], out_s...  1.95 us

profile of v3, /device:TPU:1, one launch (start us, length us, event | category | flops | bytes accessed | tf_op | source)
XLA Modules:
  0.0 67.2 jit_solution(2770862758807763762)
XLA Ops:
  0.6 64.6 %panel.1 = (bf16[7,16384]{1,0:T(8,128)(2,1)}, f32[512,256]{1,0:T(8,128)}) custom-call(bf16[448,8192]{1,0:T(8,128)(2,1)} %tok.1, bf16[448,256]{1,0:T(8,128)(2,1)} %cot.1, bf16[512,256]{1,0:T(8,128)(2,1)} %codes.1, bf16[2,256]{1,0:T(2,128)(2,1)} %scales.1), custom_call_target="tpu_custom_call" | custom-call | tf_op jit(solution)/shard_map/panel/pallas_call | solution.py:369
  65.2 2.0 %hand_over.1 = (bf16[7,16384]{1,0:T(8,128)(2,1)}, f32[512,256]{1,0:T(8,128)}) custom-call(bf16[7,16384]{1,0:T(8,128)(2,1)} %get-tuple-element.4.act, f32[512,256]{1,0:T(8,128)} %get-tuple-element.5.wg), custom_call_target="tpu_custom_call" | custom-call | tf_op jit(solution)/shard_map/hand_over/pallas_call | solution.py:408
